TPU v7x, 512 devices: a whole 4x8x8 slice. The times are simulated.
512 devices in a mesh: gx: 32 (over x, y), gy: 16 (over z, core).
Axes of the slice: x: 4, y: 8, z: 8, core: 2. Of those that a mesh axis runs over, the one named last changes fastest.
Arguments:
- density: bfloat16 [32, 16, 8, 131072], P('gx', 'gy'), may hold values from 3.1232834e-05 to 0.050048828
- source: bfloat16 [32, 16, 8, 131072], P('gx', 'gy'), may hold values from 0.5 to 4
- occupancy: int32 [32, 16, 1024], P('gx', 'gy'), may hold values from 0 to 1, as said below
- row_order: int32 [16], replicated, may hold values from 0 to 15, each once
- col_order: int32 [32], replicated, may hold values from 0 to 31, each once
Outputs:
- emission: float32 [131072], P(('gx', 'gy'))
- transmittance: float32 [131072], P(('gx', 'gy'))
Inputs may be any that keep to these rules, and one draw needn't show every extreme that they name: `occupancy`: each brick's 1 entries lie in one band of 102 consecutive blocks, counted cyclically over the 1024 blocks; the band's first and last blocks are 1.
All inputs are finite; a program needn't handle non-finite values.
Results may differ from a plain program's by a relative error of at most 0.0003.
Values sent between devices are 32-bit elements; how exact they have to be, the bound alone decides.
A program may use at most 64 MiB of HBM per device.

v0:
```python
import jax
import jax.numpy as jnp
from jax import lax
from jax.sharding import PartitionSpec as P


def composite(colors, transes, order, axis):
    shape = colors.shape[:axis] + colors.shape[axis + 1 :]

    def step(k, carry):
        total, remain = carry
        index = order[k]
        color = lax.dynamic_index_in_dim(colors, index, axis, False)
        trans = lax.dynamic_index_in_dim(transes, index, axis, False)
        return (total + remain * color, remain * trans)

    start = (jnp.zeros(shape, jnp.float32), jnp.ones(shape, jnp.float32))
    return lax.fori_loop(0, order.shape[0], step, start)


def on_device(density, source, occupancy, row_order, col_order):
    columns_count = lax.axis_size("gx")
    rows_count = lax.axis_size("gy")
    density_brick = density[0, 0]
    source_brick = source[0, 0]
    occ_blocks = occupancy[0, 0]
    occupied = occ_blocks.astype(jnp.float32)[:, None]
    depth_count, pixels = density_brick.shape
    blocks_count = occupied.shape[0]
    block_width = pixels // blocks_count
    color = jnp.zeros((blocks_count, block_width), jnp.float32)
    trans = jnp.ones((blocks_count, block_width), jnp.float32)
    for sample in range(depth_count):
        tau = (
            density_brick[sample].astype(jnp.float32).reshape(blocks_count, block_width) * occupied
        )
        fade = jnp.exp(-tau)
        color = color + trans * source_brick[sample].astype(jnp.float32).reshape(
            blocks_count, block_width
        ) * (1.0 - fade)
        trans = trans * fade
    pixel_share = pixels // (columns_count * rows_count)
    color = color.reshape(columns_count, rows_count, pixel_share)
    trans = trans.reshape(columns_count, rows_count, pixel_share)
    pieces = (
        lax.all_to_all(color, "gy", split_axis=1, concat_axis=1, tiled=True),
        lax.all_to_all(trans, "gy", split_axis=1, concat_axis=1, tiled=True),
    )
    rows_color, rows_trans = composite(pieces[0], pieces[1], row_order, 1)
    pieces = (
        lax.all_to_all(rows_color, "gx", split_axis=0, concat_axis=0, tiled=True),
        lax.all_to_all(rows_trans, "gx", split_axis=0, concat_axis=0, tiled=True),
    )
    emission, transmittance = composite(pieces[0], pieces[1], col_order, 0)
    return (emission, transmittance)


def solution(mesh):
    placed = (P("gx", "gy", None, None), P("gx", "gy", None, None), P("gx", "gy", None), P(), P())
    return jax.shard_map(
        on_device,
        mesh=mesh,
        in_specs=placed,
        out_specs=(P(("gx", "gy")), P(("gx", "gy"))),
        check_vma=False,
    )
```

profile of v0, /device:TPU:1, one launch (start us, length us, event | category | flops | bytes accessed | tf_op | source)
XLA Modules:
  0.0 279.4 jit_solution(11105812604433222320)
XLA Ops:
  0.6 41.7 %convert_reduce_fusion = (f32[131072]{0:T(1024)}, f32[131072]{0:T(1024)}, f32[131072]{0:T(1024)}, f32[131072]{0:T(1024)}, f32[131072]{0:T(1024)}, /*index=5*/f32...) fusion(bf16[1,1,8,131072]{3,2,1,0:T(8,128)(2,1)} %param.9, ...), kind=kLoop, calls=%fused_computation.8 | loop fusion | flops 2097152 | bytes 12582912 | tf_op jit(solution)/shard_map/convert_element_type | solution.py:35
  44.3 2.0 reshape.190
  46.3 2.0 reshape.191
  48.3 2.0 reshape.192
  50.3 2.0 reshape.193
  52.3 2.0 reshape.194
  54.3 2.0 reshape.195
  56.3 2.0 reshape.196
  58.3 2.0 reshape.197
  60.3 2.0 reshape.198
  62.3 2.0 reshape.199
  64.5 1.4 mul.190
  65.9 2.3 mul.191
  68.2 4.6 %multiply_multiply_fusion = (f32[32,16,256]{2,1,0:T(8,128)}, f32[32,16,256]{2,1,0:T(8,128)S(1)}) fusion(f32[32,16,256]{2,1,0:T(8,128)S(1)} %reshape.185, f32[32,16,256]{2,1,0:T(8,128)} %mul.191, f32[32,16,256]{2,1,0:T(8,128)S(1)} %reshape.187, f32[32,16,256]{2,1,0:T(8,128)S(1)} %reshape.189, f32[32,16,256]{2,1,0:T(8,128)} %reshape.191, ...), kind=kLoop, calls=%fused_computation.33 | loop fusion | flops 6946816 | bytes 9961472 | tf_op jit(solution)/shard_map/mul | solution.py:41
  73.9 11.8 %all-to-all-start = ((f32[32,16,256]{2,0,1:T(8,128)}), f32[32,16,256]{2,0,1:T(8,128)S(1)}, u32[]{:S(2)}, u32[]{:S(2)}) async-start(f32[32,16,256]{2,0,1:T(8,128)} %copy.10), calls=%async_computation | async-start | bytes 1048576 | tf_op jit(solution)/shard_map/all_to_all | solution.py:46
  86.8 16.2 %all-to-all-done = f32[32,16,256]{2,0,1:T(8,128)S(1)} async-done(((f32[32,16,256]{2,0,1:T(8,128)}), f32[32,16,256]{2,0,1:T(8,128)S(1)}, u32[]{:S(2)}, u32[]{:S(2)}) %all-to-all-start) | async-done | bytes 524320 | tf_op jit(solution)/shard_map/all_to_all | solution.py:46
  103.0 3.5 %all-to-all-start.1 = ((f32[32,16,256]{2,0,1:T(8,128)}), f32[32,16,256]{2,0,1:T(8,128)S(1)}, u32[]{:S(2)}, u32[]{:S(2)}) async-start(f32[32,16,256]{2,0,1:T(8,128)} %copy.11), calls=%async_computation.1 | async-start | bytes 1048576 | tf_op jit(solution)/shard_map/all_to_all | solution.py:47
  106.5 16.7 %all-to-all-done.1 = f32[32,16,256]{2,0,1:T(8,128)S(1)} async-done(((f32[32,16,256]{2,0,1:T(8,128)}), f32[32,16,256]{2,0,1:T(8,128)S(1)}, u32[]{:S(2)}, u32[]{:S(2)}) %all-to-all-start.1) | async-done | bytes 524320 | tf_op jit(solution)/shard_map/all_to_all | solution.py:47
  123.2 41.1 %while.32 = (s32[]{:T(128)}, f32[32,256]{1,0:T(8,128)S(1)}, f32[32,256]{1,0:T(8,128)S(1)}, s32[16]{0:T(128)S(1)}, f32[32,16,256]{2,0,1:T(8,128)S(1)}, /*index=5*...) while((s32[]{:T(128)}, f32[32,256]{1,0:T(8,128)S(1)}, f32[32,256]{1,0:T(8,128)S(1)}, ...), condition=%wide.region_1.2_spmd.clone, body=%wide.region_0.1_spmd.clone.sunk | while | flops 40966 | bytes 196761 | solution.py:18
  165.0 9.7 %all-to-all-start.3 = ((f32[32,1,256]{2,1,0:T(1,128)}), f32[32,1,256]{2,1,0:T(1,128)S(1)}, u32[]{:S(2)}, u32[]{:S(2)}) async-start(f32[32,1,256]{2,1,0:T(1,128)} %all_to_all.27), calls=%async_computation.3 | async-start | bytes 65536 | tf_op jit(solution)/shard_map/all_to_all | solution.py:52
  175.3 8.2 %all-to-all-done.3 = f32[32,1,256]{2,1,0:T(1,128)S(1)} async-done(((f32[32,1,256]{2,1,0:T(1,128)}), f32[32,1,256]{2,1,0:T(1,128)S(1)}, u32[]{:S(2)}, u32[]{:S(2)}) %all-to-all-start.3) | async-done | bytes 32800 | tf_op jit(solution)/shard_map/all_to_all | solution.py:52
  183.5 3.9 %all-to-all-start.2 = ((f32[32,1,256]{2,1,0:T(1,128)}), f32[32,1,256]{2,1,0:T(1,128)S(1)}, u32[]{:S(2)}, u32[]{:S(2)}) async-start(f32[32,1,256]{2,1,0:T(1,128)} %all_to_all.24), calls=%async_computation.2 | async-start | bytes 65536 | tf_op jit(solution)/shard_map/all_to_all | solution.py:51
  187.3 8.7 %all-to-all-done.2 = f32[32,1,256]{2,1,0:T(1,128)S(1)} async-done(((f32[32,1,256]{2,1,0:T(1,128)}), f32[32,1,256]{2,1,0:T(1,128)S(1)}, u32[]{:S(2)}, u32[]{:S(2)}) %all-to-all-start.2) | async-done | bytes 32800 | tf_op jit(solution)/shard_map/all_to_all | solution.py:51
  196.1 82.8 %while.33 = (s32[]{:T(128)}, f32[256]{0:T(256)S(1)}, f32[256]{0:T(256)S(1)}, s32[32]{0:T(128)S(1)}, f32[32,256]{1,0:T(8,128)S(1)}, /*index=5*/f32[32,256]{1,0:T(8,128)S(1)}, s32[]{:T(128)}, s32[]{:T(128)}, s32[]{:T(128)}) while((s32[]{:T(128)}, f32[256]{0:T(256)S(1)}, f32[256]{0:T(256)S(1)}, s32[32]{0:T(128)S(1)}, ...), condition=%wide.region_3.4_spmd.clone, body=%wide.region_2.3_spmd.clone.sunk | while | flops 1286 | bytes 10393 | solution.py:18
  (158 shorter events, 35.4 us)
Async XLA Ops:
  56.3 8.0 %copy-start.3 = (s32[1,1,1024]{2,1,0:T(1,128)S(1)}, s32[1,1,1024]{2,1,0:T(1,128)}, u32[]{:S(2)}) copy-start(s32[1,1,1024]{2,1,0:T(1,128)} %param.11) | copy-start | bytes 12292
  72.8 12.9 %copy-start = (f32[32,16,256]{2,1,0:T(8,128)S(1)}, f32[32,16,256]{2,1,0:T(8,128)}, u32[]{:S(2)}) copy-start(f32[32,16,256]{2,1,0:T(8,128)} %get-tuple-element.320) | copy-start | bytes 1572868
  72.8 50.4 %copy-start.4 = (s32[16]{0:T(128)S(1)}, s32[16]{0:T(128)}, u32[]{:S(2)}) copy-start(s32[16]{0:T(128)} %param.12) | copy-start | bytes 196
  73.9 29.2 %all-to-all-start = ((f32[32,16,256]{2,0,1:T(8,128)}), f32[32,16,256]{2,0,1:T(8,128)S(1)}, u32[]{:S(2)}, u32[]{:S(2)}) async-start(f32[32,16,256]{2,0,1:T(8,128)} %copy.10), calls=%async_computation | async-start | bytes 1048576 | tf_op jit(solution)/shard_map/all_to_all | solution.py:46
  85.7 110.4 %copy-start.5 = (s32[32]{0:T(128)S(1)}, s32[32]{0:T(128)}, u32[]{:S(2)}) copy-start(s32[32]{0:T(128)} %param.13) | copy-start | bytes 388
  103.0 20.2 %all-to-all-start.1 = ((f32[32,16,256]{2,0,1:T(8,128)}), f32[32,16,256]{2,0,1:T(8,128)S(1)}, u32[]{:S(2)}, u32[]{:S(2)}) async-start(f32[32,16,256]{2,0,1:T(8,128)} %copy.11), calls=%async_computation.1 | async-start | bytes 1048576 | tf_op jit(solution)/shard_map/all_to_all | solution.py:47
  165.0 18.5 %all-to-all-start.3 = ((f32[32,1,256]{2,1,0:T(1,128)}), f32[32,1,256]{2,1,0:T(1,128)S(1)}, u32[]{:S(2)}, u32[]{:S(2)}) async-start(f32[32,1,256]{2,1,0:T(1,128)} %all_to_all.27), calls=%async_computation.3 | async-start | bytes 65536 | tf_op jit(solution)/shard_map/all_to_all | solution.py:52
  183.5 12.6 %all-to-all-start.2 = ((f32[32,1,256]{2,1,0:T(1,128)}), f32[32,1,256]{2,1,0:T(1,128)S(1)}, u32[]{:S(2)}, u32[]{:S(2)}) async-start(f32[32,1,256]{2,1,0:T(1,128)} %all_to_all.24), calls=%async_computation.2 | async-start | bytes 65536 | tf_op jit(solution)/shard_map/all_to_all | solution.py:51
  278.8 0.6 copy-start.1
  278.9 0.6 copy-start.2
where the time goes:
time: 282 us; the launch traced here: 279 us
  loops' own time  94.7 us (34%)
  local copies, waits for them, and re-layouts  58.3 us (21%)
  waiting for transfers between devices  49.8 us (18%)
  other arithmetic  47 us (17%)
  starting transfers between devices  28.8 us (10%)
    another operation x2, loops' own time, composite(): return lax.fori_loop(0, order.shape[0], step, start)  94.7 us
    convert_element_type x1, other arithmetic, on_device(): density_brick[sample].astype(jnp.float32).reshape(blocks_count, block_width)  41.7 us
    dynamic_slice x48, local copies, waits for them, and re-layouts, step(): index = order[k]  28.1 us
    all_to_all x1, waiting for transfers between devices, on_device(): lax.all_to_all(trans, 'gy', split_axis=1, concat_axis=1, tiled=True)  16.7 us
    all_to_all x1, waiting for transfers between devices, on_device(): lax.all_to_all(color, 'gy', split_axis=1, concat_axis=1, tiled=True)  16.2 us
    all_to_all x1, starting transfers between devices, on_device(): lax.all_to_all(color, 'gy', split_axis=1, concat_axis=1, tiled=True)  11.8 us
    convert_element_type x8, local copies, waits for them, and re-layouts, on_device(): density_brick[sample].astype(jnp.float32).reshape(blocks_count, block_width)  11.5 us
    convert_element_type x8, local copies, waits for them, and re-layouts, on_device(): source_brick[sample].astype(jnp.float32).reshape(blocks_count, block_width)  10.4 us
  transfers between devices with their start and end apart: 4, of which 4 were waited for; matrix products, arithmetic and copies ran while one was open for 0% of the time, Pallas kernels for 0%

commit v1 on v0

v1 whole, which is shorter than its diff:
```python
import functools

import jax
import jax.numpy as jnp
from jax import lax
from jax.experimental import pallas as pl
from jax.experimental.pallas import tpu as pltpu
from jax.sharding import PartitionSpec as P

MESH = pl.DeviceIdType.MESH
ROWS = 16
COLS = 32
DEPTH = 8
BLOCK = 128
NBLK = 1024
PIX = NBLK * BLOCK
FOOT = 102
GROUP = NBLK // COLS
CHUNKS = 4


def kernel(
    dens_hbm,
    src_hbm,
    occ_ref,
    row_ref,
    col_ref,
    emission_ref,
    transmittance_ref,
    dens,
    src,
    dens_rows,
    src_rows,
    occ_rows,
    send1,
    recv1,
    info,
    recv_info,
    send2,
    recv2,
    load_sem,
    send_sems,
    recv_sems,
):
    gx = lax.axis_index("gx")
    gy = lax.axis_index("gy")

    width = NBLK // CHUNKS
    for part in range(CHUNKS):
        cut = pl.ds(part * width, width)
        pltpu.make_async_copy(dens_hbm.at[cut], dens.at[cut], load_sem.at[0]).start()
        pltpu.make_async_copy(src_hbm.at[cut], src.at[cut], load_sem.at[1]).start()

    barrier = pltpu.get_barrier_semaphore()

    @pl.loop(1, ROWS)
    def _(d):
        pl.semaphore_signal(
            barrier, inc=1, device_id={"gy": lax.rem(gy + d, ROWS)}, device_id_type=MESH
        )

    @pl.loop(1, COLS)
    def _(d):
        pl.semaphore_signal(
            barrier, inc=1, device_id={"gx": lax.rem(gx + d, COLS)}, device_id_type=MESH
        )

    occ = occ_ref[0]
    index = lax.broadcasted_iota(jnp.int32, (1, NBLK), 1)
    far = jnp.int32(4 * NBLK)
    low = jnp.min(jnp.where(occ > 0, index, far))
    high = jnp.min(jnp.where((occ > 0) & (index >= NBLK // 2), index, far))
    start = jnp.where((low < FOOT) & (high < far), high, low)
    pair = start >> 1
    info[...] = jnp.full((1, BLOCK), pair, jnp.int32)
    recv_info[gy] = jnp.full((1, BLOCK), pair, jnp.int32)

    def group_of(first, j, t):
        begin = (first - j + 15) >> 4
        return (t + 4 * ((begin - t + 3) >> 2)) & (COLS - 1)

    row = lax.broadcasted_iota(jnp.int32, (8, NBLK), 0)
    lane = lax.broadcasted_iota(jnp.int32, (8, NBLK), 1)
    occ_all = jnp.broadcast_to(occ.astype(jnp.float32), (8, NBLK))

    @pl.loop(0, ROWS)
    def _(j):
        block = group_of(pair, j, row >> 1) * GROUP + 2 * j + (row & 1)
        mine = jnp.sum(jnp.where(lane == block, occ_all, 0.0), axis=1, keepdims=True)
        occ_rows[j] = jnp.broadcast_to(mine, (8, BLOCK))

    pl.semaphore_wait(barrier, ROWS - 1 + COLS - 1)

    @pl.loop(1, ROWS)
    def _(d):
        pltpu.make_async_remote_copy(
            src_ref=info,
            dst_ref=recv_info.at[gy],
            send_sem=send_sems.at[0],
            recv_sem=recv_sems.at[0],
            device_id={"gy": lax.rem(gy + d, ROWS)},
            device_id_type=MESH,
        ).start()

    pltpu.make_async_copy(dens, dens, load_sem.at[0]).wait()
    pltpu.make_async_copy(src, src, load_sem.at[1]).wait()

    def shade(j):
        for t in range(4):
            group = group_of(pair, j, t)
            for h in range(2):
                k = 2 * t + h
                block = group * GROUP + 2 * j + h
                to = pl.ds(pl.multiple_of(j * 64 + k * 8, 8), 8)
                dens_rows[to, :] = dens[block].astype(jnp.float32)
                src_rows[to, :] = src[block].astype(jnp.float32)
        occupied = occ_rows[j]
        color = jnp.zeros((8, BLOCK), jnp.float32)
        trans = jnp.ones((8, BLOCK), jnp.float32)
        for s in range(DEPTH):
            cut = pl.ds(j * 64 + s, 8, stride=8)
            fade = jnp.exp(-(dens_rows[cut, :] * occupied))
            color = color + trans * src_rows[cut, :] * (1.0 - fade)
            trans = trans * fade
        return color, trans

    @pl.loop(1, ROWS)
    def _(d):
        j = lax.rem(gy + d, ROWS)
        color, trans = shade(j)
        send1[j, 0] = color
        send1[j, 1] = trans
        pltpu.make_async_remote_copy(
            src_ref=send1.at[j],
            dst_ref=recv1.at[gy],
            send_sem=send_sems.at[1],
            recv_sem=recv_sems.at[1],
            device_id={"gy": j},
            device_id_type=MESH,
        ).start()

    color, trans = shade(gy)
    recv1[gy, 0] = color
    recv1[gy, 1] = trans

    others = recv_info.at[pl.ds(0, ROWS - 1)]
    pltpu.make_async_copy(others, others, recv_sems.at[0]).wait()
    others = recv1.at[pl.ds(0, ROWS - 1)]
    pltpu.make_async_copy(others, others, recv_sems.at[1]).wait()

    t_of = lax.broadcasted_iota(jnp.int32, (8, BLOCK), 0) >> 1

    def over_row(k, carry):
        total, remain = carry
        r = row_ref[k]
        color = recv1[r, 0]
        trans = recv1[r, 1]
        first = jnp.broadcast_to(recv_info[r], (8, BLOCK))
        place = group_of(first, gy, t_of) >> 2
        new_total, new_remain = [], []
        for v in range(8):
            here = place == v
            new_total.append(total[v] + remain[v] * jnp.where(here, color, 0.0))
            new_remain.append(remain[v] * jnp.where(here, trans, 1.0))
        return tuple(new_total), tuple(new_remain)

    zeros = tuple(jnp.zeros((8, BLOCK), jnp.float32) for _ in range(8))
    ones = tuple(jnp.ones((8, BLOCK), jnp.float32) for _ in range(8))
    total, remain = lax.fori_loop(0, ROWS, over_row, (zeros, ones))
    for v in range(8):
        for t in range(4):
            send2[4 * v + t, 0] = total[v][2 * t : 2 * t + 2]
            send2[4 * v + t, 1] = remain[v][2 * t : 2 * t + 2]

    @pl.loop(1, COLS)
    def _(d):
        i = lax.rem(gx + d, COLS)
        pltpu.make_async_remote_copy(
            src_ref=send2.at[i],
            dst_ref=recv2.at[gx],
            send_sem=send_sems.at[2],
            recv_sem=recv_sems.at[2],
            device_id={"gx": i},
            device_id_type=MESH,
        ).start()

    recv2[gx] = send2[gx]
    others2 = recv2.at[pl.ds(0, COLS - 1)]
    pltpu.make_async_copy(others2, others2, recv_sems.at[2]).wait()

    def over_column(k, carry):
        total, remain = carry
        c = col_ref[k]
        return total + remain * recv2[c, 0], remain * recv2[c, 1]

    total, remain = lax.fori_loop(
        0,
        COLS,
        over_column,
        (jnp.zeros((2, BLOCK), jnp.float32), jnp.ones((2, BLOCK), jnp.float32)),
    )
    emission_ref[...] = total
    transmittance_ref[...] = remain

    others = recv_info.at[pl.ds(0, ROWS - 1)]
    pltpu.make_async_copy(others, others, send_sems.at[0]).wait()
    others = recv1.at[pl.ds(0, ROWS - 1)]
    pltpu.make_async_copy(others, others, send_sems.at[1]).wait()
    pltpu.make_async_copy(others2, others2, send_sems.at[2]).wait()


def on_device(density, source, occupancy, row_order, col_order):
    vmem = pl.BlockSpec(memory_space=pltpu.VMEM)
    smem = pl.BlockSpec(memory_space=pltpu.SMEM)
    hbm = pl.BlockSpec(memory_space=pltpu.HBM)
    out = jax.ShapeDtypeStruct((2, BLOCK), jnp.float32)
    density, source = (
        a.reshape(DEPTH, NBLK, BLOCK).transpose(1, 0, 2) for a in (density, source)
    )
    emission, transmittance = pl.pallas_call(
        kernel,
        out_shape=(out, out),
        in_specs=[hbm, hbm, vmem, smem, smem],
        out_specs=(vmem, vmem),
        scratch_shapes=[
            pltpu.VMEM((NBLK, DEPTH, BLOCK), jnp.bfloat16),
            pltpu.VMEM((NBLK, DEPTH, BLOCK), jnp.bfloat16),
            pltpu.VMEM((ROWS * 64, BLOCK), jnp.float32),
            pltpu.VMEM((ROWS * 64, BLOCK), jnp.float32),
            pltpu.VMEM((ROWS, 8, BLOCK), jnp.float32),
            pltpu.VMEM((ROWS, 2, 8, BLOCK), jnp.float32),
            pltpu.VMEM((ROWS, 2, 8, BLOCK), jnp.float32),
            pltpu.VMEM((1, BLOCK), jnp.int32),
            pltpu.VMEM((ROWS, 1, BLOCK), jnp.int32),
            pltpu.VMEM((COLS, 2, 2, BLOCK), jnp.float32),
            pltpu.VMEM((COLS, 2, 2, BLOCK), jnp.float32),
            pltpu.SemaphoreType.DMA((2,)),
            pltpu.SemaphoreType.DMA((3,)),
            pltpu.SemaphoreType.DMA((3,)),
        ],
        compiler_params=pltpu.CompilerParams(
            collective_id=0, has_side_effects=True, vmem_limit_bytes=60 * 1024 * 1024
        ),
    )(density, source, occupancy, row_order, col_order)
    return emission.reshape(2 * BLOCK), transmittance.reshape(2 * BLOCK)


def solution(mesh):
    placed = (P("gx", "gy", None, None), P("gx", "gy", None, None), P("gx", "gy", None), P(), P())
    return jax.shard_map(
        on_device,
        mesh=mesh,
        in_specs=placed,
        out_specs=(P(("gx", "gy")), P(("gx", "gy"))),
        check_vma=False,
    )
```

time: 282 us -> 31.8 us (0.11)
  loops' own time: 94.7 us -> 0 us
  local copies, waits for them, and re-layouts: 58.3 us -> 2.44 us
  waiting for transfers between devices: 49.8 us -> 0 us
  other arithmetic: 47 us -> 0 us
  starting transfers between devices: 28.8 us -> 0 us
  Pallas kernels: 0 us -> 28.6 us
    another operation x2 -> x0, loops' own time: 94.7 us -> none  [composite(): return lax.fori_loop(0, order.shape[0], step, start)]
    all_to_all x4 -> x0, waiting for transfers between devices: 49.8 us -> none  [the longest x1 16.7 us: on_device(): lax.all_to_all(trans, 'gy', split_axis=1, concat_axis=1, tiled=True)]
    convert_element_type x2 -> x0, other arithmetic: 41.7 us -> none  [the longest x1 41.7 us: on_device(): density_brick[sample].astype(jnp.float32).reshape(blocks_count, block_width)]
    all_to_all x4 -> x0, starting transfers between devices: 28.8 us -> none  [the longest x1 11.8 us: on_device(): lax.all_to_all(color, 'gy', split_axis=1, concat_axis=1, tiled=True)]
    pallas_call x0 -> x1, Pallas kernels: none -> 28.6 us  [on_device(): pl.pallas_call(kernel, out_shape=(out, out), in_specs=[hbm, hbm, vmem, sm...]
    dynamic_slice x80 -> x0, local copies, waits for them, and re-layouts: 28.5 us -> none  [the longest x48 28.1 us: step(): index = order[k]]
    convert_element_type x17 -> x0, local copies, waits for them, and re-layouts: 22.1 us -> none  [the longest x8 11.5 us: on_device(): density_brick[sample].astype(jnp.float32).reshape(blocks_count, block_width)]
    mul x49 -> x0, other arithmetic: 5.24 us -> none  [the longest x1 4.56 us: on_device(): trans = trans * fade]
  transfers between devices with their start and end apart: 4 -> 0, of which waited for: 4 -> 0; matrix products, arithmetic and copies ran while one was open for 0% -> 0% of each run, Pallas kernels for 0% -> 0%
where the time goes in v1:
time: 31.8 us; the launch traced here: 31.7 us
  Pallas kernels  28.6 us (90%)
  local copies, waits for them, and re-layouts  2.44 us (8%)
  between operations  0.64 us (2%)
    pallas_call x1, Pallas kernels, on_device(): pl.pallas_call(kernel, out_shape=(out, out), in_specs=[hbm, hbm, vmem, sm...  28.6 us
    unnamed x2, local copies, waits for them, and re-layouts  2.44 us

profile of v1, /device:TPU:1, one launch (start us, length us, event | category | flops | bytes accessed | tf_op | source)
XLA Modules:
  0.0 31.7 jit_solution(14201046902349559346)
XLA Ops:
  0.6 28.6 %shard_map.68 = (f32[2,128]{1,0:T(2,128)}, f32[2,128]{1,0:T(2,128)}) custom-call(bf16[1024,8,128]{2,1,0:T(8,128)(2,1)} %bitcast.8, bf16[1024,8,128]{2,1,0:T(8,128)(2,1)} %bitcast.9, s32[1,1,1024]{2,1,0:T(1,128)} %occ_ref.1, s32[16]{0:T(128)} %row_ref.1, s32[32]{0:T(128)} %col_ref.1), custom_call_target="tpu_custom_call" | custom-call | tf_op jit(solution)/shard_map/pallas_call | solution.py:220
  29.2 1.2 %copy.9 = f32[256]{0:T(256)} copy(f32[256]{0:T(256)} %bitcast.11) | data formatting | bytes 2048
  30.5 1.2 %copy.10 = f32[256]{0:T(256)} copy(f32[256]{0:T(256)} %bitcast.10) | data formatting | bytes 2048

commit v2 on v1

--- a/solution.py
+++ b/solution.py
@@ -16,17 +16,24 @@
 PIX = NBLK * BLOCK
 FOOT = 102
 GROUP = NBLK // COLS
-CHUNKS = 4
+
+
+def peer(me, d):
+    chip = d >> 1
+    away = ROWS // 4 + jnp.where(chip % 2 == 0, -(chip >> 1), (chip + 1) >> 1)
+    return lax.rem((me ^ (1 - (d & 1))) + 2 * away, ROWS)
 
 
 def kernel(
     dens_hbm,
     src_hbm,
+    occ_hbm,
+    row_hbm,
+    col_hbm,
+    out_ref,
     occ_ref,
     row_ref,
     col_ref,
-    emission_ref,
-    transmittance_ref,
     dens,
     src,
     dens_rows,
@@ -45,13 +52,13 @@
     gx = lax.axis_index("gx")
     gy = lax.axis_index("gy")
 
-    width = NBLK // CHUNKS
-    for part in range(CHUNKS):
-        cut = pl.ds(part * width, width)
-        pltpu.make_async_copy(dens_hbm.at[cut], dens.at[cut], load_sem.at[0]).start()
-        pltpu.make_async_copy(src_hbm.at[cut], src.at[cut], load_sem.at[1]).start()
-
     barrier = pltpu.get_barrier_semaphore()
+
+    @pl.loop(1, COLS)
+    def _(d):
+        pl.semaphore_signal(
+            barrier, inc=1, device_id={"gx": lax.rem(gx + d, COLS)}, device_id_type=MESH
+        )
 
     @pl.loop(1, ROWS)
     def _(d):
@@ -59,11 +66,19 @@
             barrier, inc=1, device_id={"gy": lax.rem(gy + d, ROWS)}, device_id_type=MESH
         )
 
-    @pl.loop(1, COLS)
-    def _(d):
-        pl.semaphore_signal(
-            barrier, inc=1, device_id={"gx": lax.rem(gx + d, COLS)}, device_id_type=MESH
-        )
+    small = [
+        pltpu.make_async_copy(occ_hbm, occ_ref, load_sem.at[2]),
+        pltpu.make_async_copy(row_hbm, row_ref, load_sem.at[3]),
+        pltpu.make_async_copy(col_hbm, col_ref, load_sem.at[4]),
+    ]
+    large = [
+        pltpu.make_async_copy(dens_hbm, dens, load_sem.at[0]),
+        pltpu.make_async_copy(src_hbm, src, load_sem.at[1]),
+    ]
+    for copy in small + large:
+        copy.start()
+
+    small[0].wait()
 
     occ = occ_ref[0]
     index = lax.broadcasted_iota(jnp.int32, (1, NBLK), 1)
@@ -91,19 +106,19 @@
 
     pl.semaphore_wait(barrier, ROWS - 1 + COLS - 1)
 
-    @pl.loop(1, ROWS)
+    @pl.loop(0, ROWS - 1)
     def _(d):
         pltpu.make_async_remote_copy(
             src_ref=info,
             dst_ref=recv_info.at[gy],
             send_sem=send_sems.at[0],
             recv_sem=recv_sems.at[0],
-            device_id={"gy": lax.rem(gy + d, ROWS)},
+            device_id={"gy": peer(gy, d)},
             device_id_type=MESH,
         ).start()
 
-    pltpu.make_async_copy(dens, dens, load_sem.at[0]).wait()
-    pltpu.make_async_copy(src, src, load_sem.at[1]).wait()
+    for copy in large:
+        copy.wait()
 
     def shade(j):
         for t in range(4):
@@ -124,9 +139,9 @@
             trans = trans * fade
         return color, trans
 
-    @pl.loop(1, ROWS)
-    def _(d):
-        j = lax.rem(gy + d, ROWS)
+    @pl.loop(0, ROWS - 1)
+    def _(d):
+        j = peer(gy, d)
         color, trans = shade(j)
         send1[j, 0] = color
         send1[j, 1] = trans
@@ -147,6 +162,9 @@
     pltpu.make_async_copy(others, others, recv_sems.at[0]).wait()
     others = recv1.at[pl.ds(0, ROWS - 1)]
     pltpu.make_async_copy(others, others, recv_sems.at[1]).wait()
+
+    small[1].wait()
+    small[2].wait()
 
     t_of = lax.broadcasted_iota(jnp.int32, (8, BLOCK), 0) >> 1
 
@@ -166,7 +184,7 @@
 
     zeros = tuple(jnp.zeros((8, BLOCK), jnp.float32) for _ in range(8))
     ones = tuple(jnp.ones((8, BLOCK), jnp.float32) for _ in range(8))
-    total, remain = lax.fori_loop(0, ROWS, over_row, (zeros, ones))
+    total, remain = lax.fori_loop(0, ROWS, over_row, (zeros, ones), unroll=4)
     for v in range(8):
         for t in range(4):
             send2[4 * v + t, 0] = total[v][2 * t : 2 * t + 2]
@@ -198,9 +216,10 @@
         COLS,
         over_column,
         (jnp.zeros((2, BLOCK), jnp.float32), jnp.ones((2, BLOCK), jnp.float32)),
+        unroll=8,
     )
-    emission_ref[...] = total
-    transmittance_ref[...] = remain
+    out_ref[0] = total
+    out_ref[1] = remain
 
     others = recv_info.at[pl.ds(0, ROWS - 1)]
     pltpu.make_async_copy(others, others, send_sems.at[0]).wait()
@@ -209,20 +228,26 @@
     pltpu.make_async_copy(others2, others2, send_sems.at[2]).wait()
 
 
+def deliver(both_ref, emission_ref, transmittance_ref):
+    emission_ref[...] = both_ref[0]
+    transmittance_ref[...] = both_ref[1]
+
+
 def on_device(density, source, occupancy, row_order, col_order):
     vmem = pl.BlockSpec(memory_space=pltpu.VMEM)
-    smem = pl.BlockSpec(memory_space=pltpu.SMEM)
     hbm = pl.BlockSpec(memory_space=pltpu.HBM)
-    out = jax.ShapeDtypeStruct((2, BLOCK), jnp.float32)
     density, source = (
         a.reshape(DEPTH, NBLK, BLOCK).transpose(1, 0, 2) for a in (density, source)
     )
-    emission, transmittance = pl.pallas_call(
+    both = pl.pallas_call(
         kernel,
-        out_shape=(out, out),
-        in_specs=[hbm, hbm, vmem, smem, smem],
-        out_specs=(vmem, vmem),
+        out_shape=jax.ShapeDtypeStruct((2, 2, BLOCK), jnp.float32),
+        in_specs=[hbm] * 5,
+        out_specs=vmem,
         scratch_shapes=[
+            pltpu.VMEM((1, 1, NBLK), jnp.int32),
+            pltpu.SMEM((ROWS,), jnp.int32),
+            pltpu.SMEM((COLS,), jnp.int32),
             pltpu.VMEM((NBLK, DEPTH, BLOCK), jnp.bfloat16),
             pltpu.VMEM((NBLK, DEPTH, BLOCK), jnp.bfloat16),
             pltpu.VMEM((ROWS * 64, BLOCK), jnp.float32),
@@ -234,7 +259,7 @@
             pltpu.VMEM((ROWS, 1, BLOCK), jnp.int32),
             pltpu.VMEM((COLS, 2, 2, BLOCK), jnp.float32),
             pltpu.VMEM((COLS, 2, 2, BLOCK), jnp.float32),
-            pltpu.SemaphoreType.DMA((2,)),
+            pltpu.SemaphoreType.DMA((5,)),
             pltpu.SemaphoreType.DMA((3,)),
             pltpu.SemaphoreType.DMA((3,)),
         ],
@@ -242,6 +267,10 @@
             collective_id=0, has_side_effects=True, vmem_limit_bytes=60 * 1024 * 1024
         ),
     )(density, source, occupancy, row_order, col_order)
+    out = jax.ShapeDtypeStruct((2, BLOCK), jnp.float32)
+    emission, transmittance = pl.pallas_call(
+        deliver, out_shape=(out, out), in_specs=[vmem], out_specs=(vmem, vmem)
+    )(both)
     return emission.reshape(2 * BLOCK), transmittance.reshape(2 * BLOCK)
 
 

time: 31.8 us -> 30 us (0.943)
  local copies, waits for them, and re-layouts: 2.44 us -> 0 us
  Pallas kernels: 28.6 us -> 29.1 us
    unnamed x2 -> x0, local copies, waits for them, and re-layouts: 2.44 us -> none
    pallas_call x1 -> x2, Pallas kernels: 28.6 us -> 29.1 us  [the longest x1 27.9 us: on_device(): pl.pallas_call(kernel, out_shape=jax.ShapeDtypeStruct((2, 2, BLOCK), jnp....]
where the time goes in v2:
time: 30 us; the launch traced here: 29.8 us
  Pallas kernels  29.1 us (97%)
  between operations  0.64 us (2%)
    pallas_call x1, Pallas kernels, on_device(): pl.pallas_call(kernel, out_shape=jax.ShapeDtypeStruct((2, 2, BLOCK), jnp....  27.9 us
    pallas_call x1, Pallas kernels, on_device(): pl.pallas_call(deliver, out_shape=(out, out), in_specs=[vmem], out_specs=...  1.24 us

profile of v2, /device:TPU:1, one launch (start us, length us, event | category | flops | bytes accessed | tf_op | source)
XLA Modules:
  0.0 29.8 jit_solution(16677686930511643127)
XLA Ops:
  0.6 27.9 %shard_map.68.both_ref = f32[2,2,128]{2,1,0:T(2,128)} custom-call(bf16[1024,8,128]{2,1,0:T(8,128)(2,1)} %bitcast.8, bf16[1024,8,128]{2,1,0:T(8,128)(2,1)} %bitcast.9, s32[1,1,1024]{2,1,0:T(1,128)} %occ_hbm.1, s32[16]{0:T(128)} %row_hbm.1, s32[32]{0:T(128)} %col_hbm.1), custom_call_target="tpu_custom_call" | custom-call | tf_op jit(solution)/shard_map/pallas_call | solution.py:242
  28.5 1.2 %shard_map.69 = (f32[2,128]{1,0:T(2,128)}, f32[2,128]{1,0:T(2,128)}) custom-call(f32[2,2,128]{2,1,0:T(2,128)} %shard_map.68.both_ref), custom_call_target="tpu_custom_call" | custom-call | tf_op jit(solution)/shard_map/pallas_call | solution.py:271

commit v3 on v2

--- a/solution.py
+++ b/solution.py
@@ -22,6 +22,13 @@
     chip = d >> 1
     away = ROWS // 4 + jnp.where(chip % 2 == 0, -(chip >> 1), (chip + 1) >> 1)
     return lax.rem((me ^ (1 - (d & 1))) + 2 * away, ROWS)
+
+
+def column_peer(me, d):
+    turn, dy = d & 3, d >> 2
+    dx = jnp.where(turn < 2, 2 - turn, 9 - 3 * turn)
+    dy = 4 + jnp.where(dy % 2 == 0, -(dy >> 1), (dy + 1) >> 1)
+    return ((((me >> 3) + dx) & 3) << 3) + (((me & 7) + dy) & 7)
 
 
 def kernel(
@@ -52,20 +59,6 @@
     gx = lax.axis_index("gx")
     gy = lax.axis_index("gy")
 
-    barrier = pltpu.get_barrier_semaphore()
-
-    @pl.loop(1, COLS)
-    def _(d):
-        pl.semaphore_signal(
-            barrier, inc=1, device_id={"gx": lax.rem(gx + d, COLS)}, device_id_type=MESH
-        )
-
-    @pl.loop(1, ROWS)
-    def _(d):
-        pl.semaphore_signal(
-            barrier, inc=1, device_id={"gy": lax.rem(gy + d, ROWS)}, device_id_type=MESH
-        )
-
     small = [
         pltpu.make_async_copy(occ_hbm, occ_ref, load_sem.at[2]),
         pltpu.make_async_copy(row_hbm, row_ref, load_sem.at[3]),
@@ -78,6 +71,20 @@
     for copy in small + large:
         copy.start()
 
+    barrier = pltpu.get_barrier_semaphore()
+
+    @pl.loop(1, COLS)
+    def _(d):
+        pl.semaphore_signal(
+            barrier, inc=1, device_id={"gx": lax.rem(gx + d, COLS)}, device_id_type=MESH
+        )
+
+    @pl.loop(1, ROWS)
+    def _(d):
+        pl.semaphore_signal(
+            barrier, inc=1, device_id={"gy": lax.rem(gy + d, ROWS)}, device_id_type=MESH
+        )
+
     small[0].wait()
 
     occ = occ_ref[0]
@@ -94,14 +101,20 @@
         begin = (first - j + 15) >> 4
         return (t + 4 * ((begin - t + 3) >> 2)) & (COLS - 1)
 
-    row = lax.broadcasted_iota(jnp.int32, (8, NBLK), 0)
-    lane = lax.broadcasted_iota(jnp.int32, (8, NBLK), 1)
-    occ_all = jnp.broadcast_to(occ.astype(jnp.float32), (8, NBLK))
-
-    @pl.loop(0, ROWS)
+    row = lax.broadcasted_iota(jnp.int32, (8, BLOCK), 0)
+    lane = lax.broadcasted_iota(jnp.int32, (8, BLOCK), 1)
+    occ_parts = [
+        jnp.broadcast_to(occ[:, c : c + BLOCK], (8, BLOCK)).astype(jnp.float32)
+        for c in range(0, NBLK, BLOCK)
+    ]
+
+    @pl.loop(0, ROWS, unroll=4)
     def _(j):
         block = group_of(pair, j, row >> 1) * GROUP + 2 * j + (row & 1)
-        mine = jnp.sum(jnp.where(lane == block, occ_all, 0.0), axis=1, keepdims=True)
+        mine = jnp.zeros((8, BLOCK), jnp.float32)
+        for c, part in enumerate(occ_parts):
+            mine = mine + jnp.where(lane == block - c * BLOCK, part, 0.0)
+        mine = jnp.sum(mine, axis=1, keepdims=True)
         occ_rows[j] = jnp.broadcast_to(mine, (8, BLOCK))
 
     pl.semaphore_wait(barrier, ROWS - 1 + COLS - 1)
@@ -190,9 +203,9 @@
             send2[4 * v + t, 0] = total[v][2 * t : 2 * t + 2]
             send2[4 * v + t, 1] = remain[v][2 * t : 2 * t + 2]
 
-    @pl.loop(1, COLS)
-    def _(d):
-        i = lax.rem(gx + d, COLS)
+    @pl.loop(0, COLS - 1)
+    def _(d):
+        i = column_peer(gx, d)
         pltpu.make_async_remote_copy(
             src_ref=send2.at[i],
             dst_ref=recv2.at[gx],
@@ -239,9 +252,13 @@
     density, source = (
         a.reshape(DEPTH, NBLK, BLOCK).transpose(1, 0, 2) for a in (density, source)
     )
+    operands = [
+        pltpu.with_memory_space_constraint(a, pltpu.HBM)
+        for a in (density, source, occupancy, row_order, col_order)
+    ]
     both = pl.pallas_call(
         kernel,
-        out_shape=jax.ShapeDtypeStruct((2, 2, BLOCK), jnp.float32),
+        out_shape=pltpu.VMEM((2, 2, BLOCK), jnp.float32),
         in_specs=[hbm] * 5,
         out_specs=vmem,
         scratch_shapes=[
@@ -264,12 +281,16 @@
             pltpu.SemaphoreType.DMA((3,)),
         ],
         compiler_params=pltpu.CompilerParams(
-            collective_id=0, has_side_effects=True, vmem_limit_bytes=60 * 1024 * 1024
+            collective_id=0, has_side_effects=True, vmem_limit_bytes=40 * 1024 * 1024
         ),
-    )(density, source, occupancy, row_order, col_order)
+    )(*operands)
     out = jax.ShapeDtypeStruct((2, BLOCK), jnp.float32)
     emission, transmittance = pl.pallas_call(
-        deliver, out_shape=(out, out), in_specs=[vmem], out_specs=(vmem, vmem)
+        deliver,
+        out_shape=(out, out),
+        in_specs=[vmem],
+        out_specs=(vmem, vmem),
+        compiler_params=pltpu.CompilerParams(vmem_limit_bytes=2**20),
     )(both)
     return emission.reshape(2 * BLOCK), transmittance.reshape(2 * BLOCK)
 

time: 30 us -> 28.2 us (0.940)
  Pallas kernels: 29.1 us -> 27.4 us
    pallas_call x1, Pallas kernels: 27.9 us -> 26.9 us  [on_device(): pl.pallas_call(kernel, out_shape=pltpu.VMEM((2, 2, BLOCK), jnp.float32),...]
    pallas_call x1, Pallas kernels: 1.24 us -> 0.57 us  [on_device(): pl.pallas_call(deliver, out_shape=(out, out), in_specs=[vmem], out_specs=...]
where the time goes in v3:
time: 28.2 us; the launch traced here: 28.1 us
  Pallas kernels  27.4 us (97%)
  between operations  0.64 us (2%)
    pallas_call x1, Pallas kernels, on_device(): pl.pallas_call(kernel, out_shape=pltpu.VMEM((2, 2, BLOCK), jnp.float32),...  26.9 us
    pallas_call x1, Pallas kernels, on_device(): pl.pallas_call(deliver, out_shape=(out, out), in_specs=[vmem], out_specs=...  0.57 us

profile of v3, /device:TPU:1, one launch (start us, length us, event | category | flops | bytes accessed | tf_op | source)
XLA Modules:
  0.0 28.1 jit_solution(6265692439952867210)
XLA Ops:
  0.6 26.9 %shard_map.68.both_ref = f32[2,2,128]{2,1,0:T(2,128)S(1)} custom-call(bf16[1024,8,128]{2,1,0:T(8,128)(2,1)} %bitcast.8, bf16[1024,8,128]{2,1,0:T(8,128)(2,1)} %bitcast.9, s32[1,1,1024]{2,1,0:T(1,128)} %occ_hbm.1, s32[16]{0:T(128)} %row_hbm.1, s32[32]{0:T(128)} %col_hbm.1), custom_call_target="tpu_custom_call" | custom-call | tf_op jit(solution)/shard_map/pallas_call | solution.py:259
  27.5 0.6 %shard_map.69 = (f32[2,128]{1,0:T(2,128)}, f32[2,128]{1,0:T(2,128)}) custom-call(f32[2,2,128]{2,1,0:T(2,128)S(1)} %shard_map.68.both_ref), custom_call_target="tpu_custom_call" | custom-call | tf_op jit(solution)/shard_map/pallas_call | solution.py:288

commit v4 on v3

--- a/solution.py
+++ b/solution.py
@@ -10,18 +10,13 @@
 MESH = pl.DeviceIdType.MESH
 ROWS = 16
 COLS = 32
+HALF = ROWS // 2
 DEPTH = 8
 BLOCK = 128
 NBLK = 1024
 PIX = NBLK * BLOCK
 FOOT = 102
 GROUP = NBLK // COLS
-
-
-def peer(me, d):
-    chip = d >> 1
-    away = ROWS // 4 + jnp.where(chip % 2 == 0, -(chip >> 1), (chip + 1) >> 1)
-    return lax.rem((me ^ (1 - (d & 1))) + 2 * away, ROWS)
 
 
 def column_peer(me, d):
@@ -55,9 +50,21 @@
     load_sem,
     send_sems,
     recv_sems,
+    late_sem,
+    go_sem,
 ):
     gx = lax.axis_index("gx")
     gy = lax.axis_index("gy")
+
+    barrier = pltpu.get_barrier_semaphore()
+
+    @pl.when(gy < HALF)
+    def _():
+        @pl.loop(1, ROWS)
+        def _(d):
+            pl.semaphore_signal(
+                barrier, inc=1, device_id={"gy": lax.rem(gy + d, ROWS)}, device_id_type=MESH
+            )
 
     small = [
         pltpu.make_async_copy(occ_hbm, occ_ref, load_sem.at[2]),
@@ -71,18 +78,10 @@
     for copy in small + large:
         copy.start()
 
-    barrier = pltpu.get_barrier_semaphore()
-
-    @pl.loop(1, COLS)
+    @pl.loop(0, COLS - 1)
     def _(d):
         pl.semaphore_signal(
-            barrier, inc=1, device_id={"gx": lax.rem(gx + d, COLS)}, device_id_type=MESH
-        )
-
-    @pl.loop(1, ROWS)
-    def _(d):
-        pl.semaphore_signal(
-            barrier, inc=1, device_id={"gy": lax.rem(gy + d, ROWS)}, device_id_type=MESH
+            barrier, inc=1, device_id={"gx": column_peer(gx, d)}, device_id_type=MESH
         )
 
     small[0].wait()
@@ -117,18 +116,13 @@
         mine = jnp.sum(mine, axis=1, keepdims=True)
         occ_rows[j] = jnp.broadcast_to(mine, (8, BLOCK))
 
-    pl.semaphore_wait(barrier, ROWS - 1 + COLS - 1)
-
-    @pl.loop(0, ROWS - 1)
-    def _(d):
-        pltpu.make_async_remote_copy(
-            src_ref=info,
-            dst_ref=recv_info.at[gy],
-            send_sem=send_sems.at[0],
-            recv_sem=recv_sems.at[0],
-            device_id={"gy": peer(gy, d)},
-            device_id_type=MESH,
-        ).start()
+    pl.semaphore_wait(barrier, COLS - 1 + jnp.where(gy < HALF, HALF - 1, HALF))
+
+    @pl.when(gy >= HALF)
+    def _():
+        @pl.loop(0, HALF)
+        def _(j):
+            pl.semaphore_signal(late_sem, inc=1, device_id={"gy": j}, device_id_type=MESH)
 
     for copy in large:
         copy.wait()
@@ -152,30 +146,55 @@
             trans = trans * fade
         return color, trans
 
-    @pl.loop(0, ROWS - 1)
-    def _(d):
-        j = peer(gy, d)
+    def send(j):
+        @pl.when(j != gy)
+        def _():
+            for part, (ours, theirs) in enumerate(((send1.at[j], recv1), (info, recv_info))):
+                pltpu.make_async_remote_copy(
+                    src_ref=ours,
+                    dst_ref=theirs.at[gy],
+                    send_sem=send_sems.at[part],
+                    recv_sem=recv_sems.at[part],
+                    device_id={"gy": j},
+                    device_id_type=MESH,
+                ).start()
+
+    def peer(d, half):
+        return half * HALF + (lax.rem(gy, HALF) ^ (HALF - 1 - d))
+
+    @pl.loop(0, HALF)
+    def _(d):
+        j = peer(d, 0)
         color, trans = shade(j)
         send1[j, 0] = color
         send1[j, 1] = trans
-        pltpu.make_async_remote_copy(
-            src_ref=send1.at[j],
-            dst_ref=recv1.at[gy],
-            send_sem=send_sems.at[1],
-            recv_sem=recv_sems.at[1],
-            device_id={"gy": j},
-            device_id_type=MESH,
-        ).start()
-
-    color, trans = shade(gy)
-    recv1[gy, 0] = color
-    recv1[gy, 1] = trans
-
-    others = recv_info.at[pl.ds(0, ROWS - 1)]
-    pltpu.make_async_copy(others, others, recv_sems.at[0]).wait()
-    others = recv1.at[pl.ds(0, ROWS - 1)]
-    pltpu.make_async_copy(others, others, recv_sems.at[1]).wait()
-
+        send(j)
+
+    @pl.loop(0, HALF)
+    def _(d):
+        j = peer(d, 1)
+        color, trans = shade(j)
+        send1[j, 0] = color
+        send1[j, 1] = trans
+
+    @pl.when(gy < HALF)
+    def _():
+        pl.semaphore_wait(late_sem, HALF)
+        pl.semaphore_signal(go_sem, inc=1, device_id={"gy": gy + HALF}, device_id_type=MESH)
+
+    @pl.when(gy >= HALF)
+    def _():
+        pl.semaphore_wait(go_sem, 1)
+
+    @pl.loop(0, HALF)
+    def _(d):
+        send(peer(d, 1))
+
+    recv1[gy] = send1[gy]
+
+    for part, ref in enumerate((recv1, recv_info)):
+        others = ref.at[pl.ds(0, ROWS - 1)]
+        pltpu.make_async_copy(others, others, recv_sems.at[part]).wait()
     small[1].wait()
     small[2].wait()
 
@@ -234,10 +253,9 @@
     out_ref[0] = total
     out_ref[1] = remain
 
-    others = recv_info.at[pl.ds(0, ROWS - 1)]
-    pltpu.make_async_copy(others, others, send_sems.at[0]).wait()
-    others = recv1.at[pl.ds(0, ROWS - 1)]
-    pltpu.make_async_copy(others, others, send_sems.at[1]).wait()
+    for part, ref in enumerate((recv1, recv_info)):
+        others = ref.at[pl.ds(0, ROWS - 1)]
+        pltpu.make_async_copy(others, others, send_sems.at[part]).wait()
     pltpu.make_async_copy(others2, others2, send_sems.at[2]).wait()
 
 
@@ -279,6 +297,8 @@
             pltpu.SemaphoreType.DMA((5,)),
             pltpu.SemaphoreType.DMA((3,)),
             pltpu.SemaphoreType.DMA((3,)),
+            pltpu.SemaphoreType.REGULAR,
+            pltpu.SemaphoreType.REGULAR,
         ],
         compiler_params=pltpu.CompilerParams(
             collective_id=0, has_side_effects=True, vmem_limit_bytes=40 * 1024 * 1024

time: 28.2 us -> 26.6 us (0.943)
  Pallas kernels: 27.4 us -> 25.9 us
    pallas_call x1, Pallas kernels: 26.9 us -> 25.3 us  [on_device(): pl.pallas_call(kernel, out_shape=pltpu.VMEM((2, 2, BLOCK), jnp.float32),...]
where the time goes in v4:
time: 26.6 us; the launch traced here: 26.5 us
  Pallas kernels  25.9 us (97%)
  between operations  0.64 us (2%)
    pallas_call x1, Pallas kernels, on_device(): pl.pallas_call(kernel, out_shape=pltpu.VMEM((2, 2, BLOCK), jnp.float32),...  25.3 us
    pallas_call x1, Pallas kernels, on_device(): pl.pallas_call(deliver, out_shape=(out, out), in_specs=[vmem], out_specs=...  0.57 us

profile of v4, /device:TPU:1, one launch (start us, length us, event | category | flops | bytes accessed | tf_op | source)
XLA Modules:
  0.0 26.5 jit_solution(13990882442766029344)
XLA Ops:
  0.6 25.3 %shard_map.68.both_ref = f32[2,2,128]{2,1,0:T(2,128)S(1)} custom-call(bf16[1024,8,128]{2,1,0:T(8,128)(2,1)} %bitcast.8, bf16[1024,8,128]{2,1,0:T(8,128)(2,1)} %bitcast.9, s32[1,1,1024]{2,1,0:T(1,128)} %occ_hbm.1, s32[16]{0:T(128)} %row_hbm.1, s32[32]{0:T(128)} %col_hbm.1), custom_call_target="tpu_custom_call" | custom-call | tf_op jit(solution)/shard_map/pallas_call | solution.py:277
  25.9 0.6 %shard_map.69 = (f32[2,128]{1,0:T(2,128)}, f32[2,128]{1,0:T(2,128)}) custom-call(f32[2,2,128]{2,1,0:T(2,128)S(1)} %shard_map.68.both_ref), custom_call_target="tpu_custom_call" | custom-call | tf_op jit(solution)/shard_map/pallas_call | solution.py:308

commit v5 on v4

--- a/solution.py
+++ b/solution.py
@@ -11,6 +11,7 @@
 ROWS = 16
 COLS = 32
 HALF = ROWS // 2
+HUB = 8
 DEPTH = 8
 BLOCK = 128
 NBLK = 1024
@@ -52,19 +53,13 @@
     recv_sems,
     late_sem,
     go_sem,
+    row_sem,
+    row_go_sem,
 ):
     gx = lax.axis_index("gx")
     gy = lax.axis_index("gy")
 
     barrier = pltpu.get_barrier_semaphore()
-
-    @pl.when(gy < HALF)
-    def _():
-        @pl.loop(1, ROWS)
-        def _(d):
-            pl.semaphore_signal(
-                barrier, inc=1, device_id={"gy": lax.rem(gy + d, ROWS)}, device_id_type=MESH
-            )
 
     small = [
         pltpu.make_async_copy(occ_hbm, occ_ref, load_sem.at[2]),
@@ -75,14 +70,26 @@
         pltpu.make_async_copy(dens_hbm, dens, load_sem.at[0]),
         pltpu.make_async_copy(src_hbm, src, load_sem.at[1]),
     ]
-    for copy in small + large:
+    for copy in small:
         copy.start()
-
-    @pl.loop(0, COLS - 1)
-    def _(d):
-        pl.semaphore_signal(
-            barrier, inc=1, device_id={"gx": column_peer(gx, d)}, device_id_type=MESH
-        )
+    for at in range(0, NBLK, NBLK // 4):
+        cut = pl.ds(at, NBLK // 4)
+        pltpu.make_async_copy(dens_hbm.at[cut], dens.at[cut], load_sem.at[0]).start()
+        pltpu.make_async_copy(src_hbm.at[cut], src.at[cut], load_sem.at[1]).start()
+
+    @pl.when(gy < HALF)
+    def _():
+        @pl.loop(1, ROWS)
+        def _(d):
+            pl.semaphore_signal(
+                barrier, inc=1, device_id={"gy": lax.rem(gy + d, ROWS)}, device_id_type=MESH
+            )
+
+    @pl.when(gx == HUB)
+    def _():
+        @pl.loop(1, COLS)
+        def _(i):
+            pl.semaphore_signal(barrier, inc=1, device_id={"gx": lax.rem(HUB + i, COLS)}, device_id_type=MESH)
 
     small[0].wait()
 
@@ -116,7 +123,13 @@
         mine = jnp.sum(mine, axis=1, keepdims=True)
         occ_rows[j] = jnp.broadcast_to(mine, (8, BLOCK))
 
-    pl.semaphore_wait(barrier, COLS - 1 + jnp.where(gy < HALF, HALF - 1, HALF))
+    pl.semaphore_wait(
+        barrier, jnp.where(gx == HUB, 0, 1) + jnp.where(gy < HALF, HALF - 1, HALF)
+    )
+
+    @pl.when(gx != HUB)
+    def _():
+        pl.semaphore_signal(row_sem, inc=1, device_id={"gx": HUB}, device_id_type=MESH)
 
     @pl.when(gy >= HALF)
     def _():
@@ -192,6 +205,14 @@
 
     recv1[gy] = send1[gy]
 
+    @pl.when(gx == HUB)
+    def _():
+        pl.semaphore_wait(row_sem, COLS - 1)
+
+        @pl.loop(1, COLS)
+        def _(i):
+            pl.semaphore_signal(row_go_sem, inc=1, device_id={"gx": lax.rem(HUB + i, COLS)}, device_id_type=MESH)
+
     for part, ref in enumerate((recv1, recv_info)):
         others = ref.at[pl.ds(0, ROWS - 1)]
         pltpu.make_async_copy(others, others, recv_sems.at[part]).wait()
@@ -221,6 +242,10 @@
         for t in range(4):
             send2[4 * v + t, 0] = total[v][2 * t : 2 * t + 2]
             send2[4 * v + t, 1] = remain[v][2 * t : 2 * t + 2]
+
+    @pl.when(gx != HUB)
+    def _():
+        pl.semaphore_wait(row_go_sem, 1)
 
     @pl.loop(0, COLS - 1)
     def _(d):
@@ -299,6 +324,8 @@
             pltpu.SemaphoreType.DMA((3,)),
             pltpu.SemaphoreType.REGULAR,
             pltpu.SemaphoreType.REGULAR,
+            pltpu.SemaphoreType.REGULAR,
+            pltpu.SemaphoreType.REGULAR,
         ],
         compiler_params=pltpu.CompilerParams(
             collective_id=0, has_side_effects=True, vmem_limit_bytes=40 * 1024 * 1024

time: 26.6 us -> 26.6 us (level)
  no operation moved by 1% of the time
where the time goes in v5:
time: 26.6 us; the launch traced here: 26.4 us
  Pallas kernels  25.8 us (97%)
  between operations  0.64 us (2%)
    pallas_call x1, Pallas kernels, on_device(): pl.pallas_call(kernel, out_shape=pltpu.VMEM((2, 2, BLOCK), jnp.float32),...  25.2 us
    pallas_call x1, Pallas kernels, on_device(): pl.pallas_call(deliver, out_shape=(out, out), in_specs=[vmem], out_specs=...  0.57 us

profile of v5, /device:TPU:1, one launch (start us, length us, event | category | flops | bytes accessed | tf_op | source)
XLA Modules:
  0.0 26.4 jit_solution(3652186381191657723)
XLA Ops:
  0.6 25.2 %shard_map.68.both_ref = f32[2,2,128]{2,1,0:T(2,128)S(1)} custom-call(bf16[1024,8,128]{2,1,0:T(8,128)(2,1)} %bitcast.8, bf16[1024,8,128]{2,1,0:T(8,128)(2,1)} %bitcast.9, s32[1,1,1024]{2,1,0:T(1,128)} %occ_hbm.1, s32[16]{0:T(128)} %row_hbm.1, s32[32]{0:T(128)} %col_hbm.1), custom_call_target="tpu_custom_call" | custom-call | tf_op jit(solution)/shard_map/pallas_call | solution.py:302
  25.9 0.6 %shard_map.69 = (f32[2,128]{1,0:T(2,128)}, f32[2,128]{1,0:T(2,128)}) custom-call(f32[2,2,128]{2,1,0:T(2,128)S(1)} %shard_map.68.both_ref), custom_call_target="tpu_custom_call" | custom-call | tf_op jit(solution)/shard_map/pallas_call | solution.py:335
